TPU v7x, 32 devices: a whole 2x2x4 slice. The times are simulated.
32 devices in a mesh: groups: 2 (over x), blk: 16 (over z, y, core).
Axes of the slice: x: 2, y: 2, z: 4, core: 2. Of those that a mesh axis runs over, the one named last changes fastest.
Arguments:
- mesh_in: bfloat16 [8192, 512], P(('groups', 'blk')), parts along dimension 0, may hold values from -40 to 40
- grid_in: bfloat16 [4096, 512], P(('groups', 'blk')), parts along dimension 0, may hold values from -6 to 6
- cotangent: bfloat16 [4096, 512], P(('groups', 'blk')), parts along dimension 0, may hold values from -6 to 6
- w_send: bfloat16 [512, 512], replicated, may hold values from -0.25 to 0.25
- w_self: bfloat16 [512, 512], replicated, may hold values from -0.25 to 0.25
- w_out: bfloat16 [512, 512], replicated, may hold values from -0.25 to 0.25
- w_src: bfloat16 [512, 512], replicated, may hold values from -0.25 to 0.25
- w_dst: bfloat16 [512, 512], replicated, may hold values from -0.25 to 0.25
- w_dec: bfloat16 [512, 512], replicated, may hold values from -0.25 to 0.25
- adj_blocks: bfloat16 [32, 4, 128, 128], P('blk'), may hold values from -0.25 to 0.25
- adj_index: int32 [32, 4], replicated, may hold values from 0 to 31, as said below
- src_rows: int32 [16, 5, 64], P('blk'), may hold values from 0 to 255
- dst_rows: int32 [16, 5, 64], P('blk'), may hold values from 0 to 127
- counts: int32 [16, 5], P('blk'), may hold values from 1 to 64, as said below
Outputs:
- grid_out: bfloat16 [4096, 512], P(('groups', 'blk')), parts along dimension 0
- grad_grid: bfloat16 [4096, 512], P(('groups', 'blk')), parts along dimension 0
- grad_mesh: bfloat16 [8192, 512], P(('groups', 'blk')), parts along dimension 0
There are 2 independent parts, one for each index of `groups`. A program takes and returns all parts, laid end to end along the dimension named above; an argument that names none is the same for every part. Nothing has to cross between parts.
Inputs may be any that keep to these rules, and one draw needn't show every extreme that they name: `adj_index`: column 0 names the block itself; every entry names a block on a device at cycle distance at most 2 (device indices wrap around), and every row has one entry at distance 2 on each side. `counts`: some destination has all 64 slots live from each of its 5 owners, and some owner has all 64 slots live to each of its destinations.
All inputs are finite; a program needn't handle non-finite values.
Results may differ from a plain program's by a relative error of at most 0.0085.
Values may be sent and summed in bfloat16 or wider, within the bound.
A program may use at most 64 MiB of HBM per device.

v0:
```python
import jax
import jax.numpy as jnp
from jax import lax
from jax.sharding import PartitionSpec as P

REACH = 2


def passed_along(block, axis, distance):
    devices = range(lax.axis_size(axis))
    route = [((i - distance) % len(devices), i) for i in devices]
    return lax.ppermute(block, axis, route)


def silu_grad(value):
    sig = jax.nn.sigmoid(value)
    return sig * (1.0 + value * (1.0 - sig))


def owner_index(my_src, offsets):
    held = []
    for place, offset in enumerate(offsets):
        if offset == 0:
            held.append(my_src[place])
        else:
            held.append(passed_along(my_src[place], "blk", offset))
    return held


def body(
    mesh_in,
    grid_in,
    cotangent,
    w_send,
    w_self,
    w_out,
    w_src,
    w_dst,
    w_dec,
    adj_blocks,
    adj_index,
    src_rows,
    dst_rows,
    counts,
):
    nodes = lax.axis_size("blk")
    me = lax.axis_index("blk")
    per_dev, width = mesh_in.shape
    blocks = per_dev // 128
    neighbours = adj_blocks.shape[1]
    offsets = list(range(-REACH, REACH + 1))
    h32 = mesh_in.astype(jnp.float32)
    scale = lax.rsqrt(jnp.mean(h32 * h32, axis=-1, keepdims=True) + 1e-05)
    normed = h32 * scale
    normed_b = normed.astype(jnp.bfloat16)
    sent = jnp.dot(normed_b, w_send, preferred_element_type=jnp.float32).astype(jnp.bfloat16)
    panel_list = []
    for offset in offsets:
        if offset == 0:
            panel_list.append(sent)
        else:
            panel_list.append(passed_along(sent, "blk", -offset))
    window = jnp.stack(panel_list).reshape(len(offsets) * blocks, 128, width)
    local_index = lax.dynamic_slice_in_dim(adj_index, me * blocks, blocks, 0)
    distance = (local_index // blocks - me + nodes) % nodes
    signed = jnp.where(distance > REACH, distance - nodes, distance)
    window_slot = (signed + REACH) * blocks + local_index % blocks
    picked = window[window_slot]
    agg = jnp.einsum(
        "bkij,bkjd->bid", adj_blocks, picked, preferred_element_type=jnp.float32
    ).reshape(per_dev, width)
    pre_act = jnp.dot(normed_b, w_self, preferred_element_type=jnp.float32) + agg
    act = jax.nn.silu(pre_act).astype(jnp.bfloat16)
    mesh_out = (h32 + jnp.dot(act, w_out, preferred_element_type=jnp.float32)).astype(jnp.bfloat16)
    src_proj = jnp.dot(mesh_out, w_src, preferred_element_type=jnp.float32).astype(jnp.bfloat16)
    places, slots = (src_rows.shape[1], src_rows.shape[2])
    grid_rows = grid_in.shape[0]
    my_src = src_rows[0]
    held = []
    held = owner_index(my_src, offsets)
    pieces = []
    for place, offset in enumerate(offsets):
        rows_out = src_proj[held[place]]
        if offset == 0:
            pieces.append(rows_out)
        else:
            pieces.append(passed_along(rows_out, "blk", -offset))
    incoming = jnp.concatenate(pieces, axis=0)
    live = (
        (jnp.arange(slots, dtype=jnp.int32)[None, :] < counts[0][:, None])
        .astype(jnp.float32)
        .reshape(-1, 1)
    )
    dst = dst_rows[0].reshape(-1)
    dst_proj = jnp.dot(grid_in, w_dst, preferred_element_type=jnp.float32)
    edge_pre = incoming.astype(jnp.float32) + dst_proj[dst]
    edge = jax.nn.silu(edge_pre) * live
    grid_sum = jnp.zeros((grid_rows, width), jnp.float32).at[dst].add(edge).astype(jnp.bfloat16)
    grid_out = (
        grid_in.astype(jnp.float32) + jnp.dot(grid_sum, w_dec, preferred_element_type=jnp.float32)
    ).astype(jnp.bfloat16)
    d_sum = jnp.dot(cotangent, w_dec.T, preferred_element_type=jnp.float32).astype(jnp.bfloat16)
    d_edge = (d_sum[dst].astype(jnp.float32) * silu_grad(edge_pre) * live).astype(jnp.bfloat16)
    d_dst = (
        jnp.zeros((grid_rows, width), jnp.float32)
        .at[dst]
        .add(d_edge.astype(jnp.float32))
        .astype(jnp.bfloat16)
    )
    grad_grid = (
        cotangent.astype(jnp.float32) + jnp.dot(d_dst, w_dst.T, preferred_element_type=jnp.float32)
    ).astype(jnp.bfloat16)
    d_edge_places = d_edge.reshape(places, slots, width)
    d_src_total = jnp.zeros((per_dev, width), jnp.float32)
    for place, offset in enumerate(offsets):
        if offset == 0:
            back = d_edge_places[place]
        else:
            back = passed_along(d_edge_places[place], "blk", offset)
        d_src_total = d_src_total.at[held[place]].add(back.astype(jnp.float32))
    d_src = d_src_total.astype(jnp.bfloat16)
    d_mesh = jnp.dot(d_src, w_src.T, preferred_element_type=jnp.float32)
    d_mesh_b = d_mesh.astype(jnp.bfloat16)
    d_act = jnp.dot(d_mesh_b, w_out.T, preferred_element_type=jnp.float32)
    d_pre = (d_act * silu_grad(pre_act)).astype(jnp.bfloat16)
    d_pre_blocks = d_pre.reshape(blocks, 128, width)
    contrib = jnp.einsum(
        "bkji,bid->bkjd", adj_blocks, d_pre_blocks, preferred_element_type=jnp.float32
    )
    spots = (
        jnp.arange(len(offsets) * blocks, dtype=jnp.int32)[:, None]
        == window_slot.reshape(-1)[None, :]
    ).astype(jnp.float32)
    window_grad = jnp.einsum(
        "wm,mjd->wjd",
        spots,
        contrib.reshape(blocks * neighbours, 128, width),
        precision=lax.Precision.HIGHEST,
    )
    window_grad = window_grad.reshape(len(offsets), per_dev, width)
    total = window_grad[REACH]
    for offset in offsets:
        if offset != 0:
            total = total + passed_along(
                window_grad[offset + REACH].astype(jnp.bfloat16), "blk", offset
            ).astype(jnp.float32)
    d_sent = total.astype(jnp.bfloat16)
    d_norm = jnp.dot(d_pre, w_self.T, preferred_element_type=jnp.float32) + jnp.dot(
        d_sent, w_send.T, preferred_element_type=jnp.float32
    )
    d_h = scale * (d_norm - normed * jnp.mean(d_norm * normed, axis=-1, keepdims=True))
    grad_mesh = (d_mesh + d_h).astype(jnp.bfloat16)
    return (grid_out, grad_grid, grad_mesh)


def solution(mesh):
    return jax.shard_map(
        body,
        mesh=mesh,
        in_specs=(
            P(("groups", "blk"), None),
            P(("groups", "blk"), None),
            P(("groups", "blk"), None),
            P(),
            P(),
            P(),
            P(),
            P(),
            P(),
            P("blk", None, None, None),
            P(),
            P("blk", None, None),
            P("blk", None, None),
            P("blk", None),
        ),
        out_specs=(
            P(("groups", "blk"), None),
            P(("groups", "blk"), None),
            P(("groups", "blk"), None),
        ),
        check_vma=False,
    )
```

profile of v0, /device:TPU:0, one launch (start us, length us, event | category | flops | bytes accessed | tf_op | source)
XLA Modules:
  0.0 114.4 jit_solution(10805475729856812171)
XLA Ops:
  0.7 1.2 %fusion.18 = f32[256]{0:T(256)S(1)} fusion(bf16[256,512]{1,0:T(8,128)(2,1)} %param.14), kind=kLoop, calls=%fused_computation.47 | loop fusion | flops 392960 | bytes 263168 | tf_op jit(solution)/shard_map/reduce_sum | solution.py:53
  2.0 1.3 %convolution_convert_fusion.1 = bf16[256,512]{1,0:T(8,128)(2,1)S(1)} fusion(bf16[512,512]{1,0:T(8,128)(2,1)S(1)} %copy-done, bf16[256,512]{1,0:T(8,128)(2,1)} %param.14, f32[256]{0:T(256)S(1)} %add_rsqrt_fusion), kind=kOutput, calls=%fused_computation.22 | convolution fusion | flops 134742016 | bytes 1049600 | tf_op jit(solution)/shard_map/dot_general | solution.py:56
  3.2 6.1 %collective-permute-start.3 = (bf16[256,512]{1,0:T(8,128)(2,1)S(1)}, bf16[256,512]{1,0:T(8,128)(2,1)S(1)}, u32[]{:S(2)}, u32[]{:S(2)}) collective-permute-start(bf16[256,512]{1,0:T(8,128)(2,1)S(1)} %convolution_convert_fusion.1), channel_id=1, source_target_pairs={{2,0},{3,1},{4,2},{5,3},{6,4},{7,5},{8,6},{9,7},{10,8},{11,9},{12,... | collective-permute-start | bytes 786440 | tf_op jit(solution)/shard_map/ppermute | solution.py:12
  9.3 0.5 collective-permute-start.1
  9.8 0.7 collective-permute-start
  11.1 0.3 convolution_convert_fusion.2
  11.4 0.2 fusion.68
  11.9 2.0 %gather_fusion.7 = bf16[320,512]{1,0:T(8,128)(2,1)S(1)} fusion(bf16[128,512]{1,0:T(8,128)(2,1)S(1)} %convolution_convert_fusion.2, s32[1024]{0:T(1024)S(1)} %pad_clamp_fusion), kind=kCustom, calls=%fused_computation.7 | custom fusion | bytes 656640 | tf_op jit(solution)/shard_map/gather | solution.py:103
  14.0 1.6 %gather_fusion.6 = f32[320,512]{1,0:T(8,128)S(1)} fusion(f32[128,512]{1,0:T(8,128)S(1)} %fusion.68, s32[1024]{0:T(1024)S(1)} %pad_clamp_fusion), kind=kCustom, calls=%fused_computation.6 | custom fusion | bytes 1312000 | tf_op jit(solution)/shard_map/gather | solution.py:96
  15.6 6.3 %collective-permute-done.10 = s32[64]{0:T(128)S(1)} collective-permute-done((s32[64]{0:T(128)S(1)}, s32[64]{0:T(128)S(1)}, u32[]{:S(2)}, u32[]{:S(2)}) %collective-permute-start.10) | collective-permute-done | bytes 288 | tf_op jit(solution)/shard_map/ppermute | solution.py:12
  21.9 7.8 %collective-permute-start.6 = (s32[64]{0:T(128)S(1)}, s32[64]{0:T(128)S(1)}, u32[]{:S(2)}, u32[]{:S(2)}) collective-permute-start(s32[64]{0:T(128)S(1)} %get-tuple-element.14), channel_id=1, source_target_pairs={{1,0},{2,1},{3,2},{4,3},{5,4},{6,5},{7,6},{8,7},{9,8},{10,9},{11,1... | collective-permute-start | bytes 776 | tf_op jit(solution)/shard_map/ppermute | solution.py:12
  29.8 1.3 %collective-permute-done.6 = s32[64]{0:T(128)S(1)} collective-permute-done((s32[64]{0:T(128)S(1)}, s32[64]{0:T(128)S(1)}, u32[]{:S(2)}, u32[]{:S(2)}) %collective-permute-start.6) | collective-permute-done | bytes 288 | tf_op jit(solution)/shard_map/ppermute | solution.py:12
  31.1 3.5 %collective-permute-done.4 = s32[64]{0:T(128)S(1)} collective-permute-done((s32[64]{0:T(128)S(1)}, s32[64]{0:T(128)S(1)}, u32[]{:S(2)}, u32[]{:S(2)}) %collective-permute-start.4) | collective-permute-done | bytes 288 | tf_op jit(solution)/shard_map/ppermute | solution.py:12
  34.6 1.7 %collective-permute-start.8 = (s32[64]{0:T(128)S(1)}, s32[64]{0:T(128)S(1)}, u32[]{:S(2)}, u32[]{:S(2)}) collective-permute-start(s32[64]{0:T(128)S(1)} %get-tuple-element.16), channel_id=1, source_target_pairs={{15,0},{0,1},{1,2},{2,3},{3,4},{4,5},{5,6},{6,7},{7,8},{8,9},{9,10... | collective-permute-start | bytes 776 | tf_op jit(solution)/shard_map/ppermute | solution.py:12
  36.3 5.5 %collective-permute-done.8 = s32[64]{0:T(128)S(1)} collective-permute-done((s32[64]{0:T(128)S(1)}, s32[64]{0:T(128)S(1)}, u32[]{:S(2)}, u32[]{:S(2)}) %collective-permute-start.8) | collective-permute-done | bytes 288 | tf_op jit(solution)/shard_map/ppermute | solution.py:12
  41.8 1.0 bitcast_dynamic-update-slice_fusion.4
  42.9 1.1 copy-done.9
  44.0 1.9 %gather_fusion = bf16[8,128,512]{2,1,0:T(8,128)(2,1)S(1)} fusion(bf16[10,128,512]{2,1,0:T(8,128)(2,1)} %bitcast.82, s32[1024]{0:T(1024)S(1)} %pad_clamp_fusion.6), kind=kCustom, calls=%fused_computation | custom fusion | bytes 2097184 | tf_op jit(solution)/shard_map/gather | solution.py:68
  45.9 1.3 %fusion.71 = f32[2,512,128,1]{1,2,3,0:T(8,128)S(1)} fusion(bf16[2,4,128,128]{3,2,1,0:T(8,128)(2,1)} %param.23, bf16[2,4,128,512]{3,2,1,0:T(8,128)(2,1)S(1)} %bitcast.80), kind=kOutput, calls=%fused_computation.139 | convolution fusion | flops 134217728 | bytes 1835008 | tf_op jit(solution)/shard_map/bkij,bkjd->bid/dot_general | solution.py:69
  47.3 1.1 %convolution_add_fusion.2 = f32[256,512]{1,0:T(8,128)} fusion(f32[256,512]{1,0:T(8,128)S(1)} %bitcast.81, bf16[512,512]{1,0:T(8,128)(2,1)S(1)} %copy-done.2, bf16[256,512]{1,0:T(8,128)(2,1)S(1)} %copy-done.1, f32[256]{0:T(256)S(1)} %add_rsqrt_fusion), kind=kOutput, calls=%fused_computation.18 | convolution fusion | flops 134742016 | bytes 1836032 | tf_op jit(solution)/shard_map/dot_general | solution.py:72
  48.4 1.7 %convolution_convert_fusion = bf16[256,512]{1,0:T(8,128)(2,1)S(1)} fusion(bf16[512,512]{1,0:T(8,128)(2,1)S(1)} %copy-done.14, bf16[512,512]{1,0:T(8,128)(2,1)} %param.19, bf16[256,512]{1,0:T(8,128)(2,1)S(1)} %copy-done.1, f32[256,512]{1,0:T(8,128)} %convolution_add_fusion.2), kind=kOutput, calls=%fused_computation.21 | convolution fusion | flops 269615104 | bytes 2097152 | tf_op jit(solution)/shard_map/dot_general | solution.py:75
  50.2 0.7 gather_fusion.1
  51.0 0.7 gather_fusion.5
  51.7 0.7 gather_fusion.4
  52.4 0.7 gather_fusion.3
  53.1 0.7 gather_fusion.2
  53.8 4.4 %collective-permute-start.9 = (bf16[64,512]{1,0:T(8,128)(2,1)S(1)}, bf16[64,512]{1,0:T(8,128)(2,1)S(1)}, u32[]{:S(2)}, u32[]{:S(2)}) collective-permute-start(bf16[64,512]{1,0:T(8,128)(2,1)S(1)} %gather_fusion.4), channel_id=1, source_target_pairs={{1,0},{2,1},{3,2},{4,3},{5,4},{6,5},{7,6},{8,7},{9,8},{10,9},{11,1... | collective-permute-start | bytes 196616 | tf_op jit(solution)/shard_map/ppermute | solution.py:12
  58.3 2.0 %collective-permute-start.11 = (bf16[64,512]{1,0:T(8,128)(2,1)S(1)}, bf16[64,512]{1,0:T(8,128)(2,1)S(1)}, u32[]{:S(2)}, u32[]{:S(2)}) collective-permute-start(bf16[64,512]{1,0:T(8,128)(2,1)S(1)} %gather_fusion.5), channel_id=1, source_target_pairs={{2,0},{3,1},{4,2},{5,3},{6,4},{7,5},{8,6},{9,7},{10,8},{11,9},{12,... | collective-permute-start | bytes 196616 | tf_op jit(solution)/shard_map/ppermute | solution.py:12
  60.3 0.3 collective-permute-done.9
  60.6 1.9 %collective-permute-done.11 = bf16[64,512]{1,0:T(8,128)(2,1)S(1)} collective-permute-done((bf16[64,512]{1,0:T(8,128)(2,1)S(1)}, bf16[64,512]{1,0:T(8,128)(2,1)S(1)}, u32[]{:S(2)}, u32[]{:S(2)}) %collective-permute-start.11) | collective-permute-done | bytes 65568 | tf_op jit(solution)/shard_map/ppermute | solution.py:12
  62.5 0.3 multiply_convert_fusion
  62.9 0.7 fusion.66
  63.5 4.5 %collective-permute-start.13 = (bf16[64,512]{1,0:T(8,128)(2,1)}, bf16[64,512]{1,0:T(8,128)(2,1)}, u32[]{:S(2)}, u32[]{:S(2)}) collective-permute-start(bf16[64,512]{1,0:T(8,128)(2,1)} %get-tuple-element.11), channel_id=1, source_target_pairs={{1,0},{2,1},{3,2},{4,3},{5,4},{6,5},{7,6},{8,7},{9,8},{10,9},{11,1... | collective-permute-start | bytes 196616 | tf_op jit(solution)/shard_map/ppermute | solution.py:12
  68.0 2.0 %collective-permute-start.12 = (bf16[64,512]{1,0:T(8,128)(2,1)S(1)}, bf16[64,512]{1,0:T(8,128)(2,1)}, u32[]{:S(2)}, u32[]{:S(2)}) collective-permute-start(bf16[64,512]{1,0:T(8,128)(2,1)S(1)} %get-tuple-element.12), channel_id=1, source_target_pairs={{2,0},{3,1},{4,2},{5,3},{6,4},{7,5},{8,6},{9,7},{10,8},{11,9},{12,... | collective-permute-start | bytes 196616 | tf_op jit(solution)/shard_map/ppermute | solution.py:12
  70.0 2.7 %scatter_custom_fusion = f32[128,512]{1,0:T(8,128)S(1)} fusion(s32[320]{0:T(512)S(1)} %fusion.60, f32[320,512]{1,0:T(8,128)S(1)} %gather_fusion.6, bf16[320,512]{1,0:T(8,128)(2,1)S(1)} %constant_dynamic-update-slice_fusion, f32[320]{0:T(512)S(1)} %reshape.146, f32[]{:T(128)} %constant.72.clone.1, f32[]{:T(128)} %constant.58.clone.1), kind=kCustom, calls=%fused_computation.37 | custom fusion | flops 1310720 | bytes 1247240 | tf_op jit(solution)/shard_map/scatter-add | solution.py:98
  72.8 1.8 %fusion.2 = bf16[128,512]{1,0:T(8,128)(2,1)} fusion(bf16[512,512]{1,0:T(8,128)(2,1)S(1)} %copy-done.8, bf16[128,512]{1,0:T(8,128)(2,1)} %param.15, f32[128,512]{1,0:T(8,128)S(1)} %scatter_custom_fusion), kind=kOutput, calls=%fused_computation.25 | convolution fusion | flops 67371008 | bytes 1048576 | tf_op jit(solution)/shard_map/dot_general | solution.py:100
  74.6 3.2 %scatter_custom_fusion.1 = f32[128,512]{1,0:T(8,128)} fusion(s32[320]{0:T(512)S(1)} %fusion.60, bf16[320,512]{1,0:T(8,128)(2,1)S(1)} %multiply_convert_fusion, f32[]{:T(128)} %constant.58.clone.1), kind=kCustom, calls=%fused_computation.34 | custom fusion | flops 327680 | bytes 589828 | tf_op jit(solution)/shard_map/scatter-add | solution.py:107
  77.7 1.4 %scatter_custom_fusion.2 = f32[256,512]{1,0:T(8,128)S(1)} fusion(s32[64]{0:T(128)} %copy-done.28, f32[]{:T(128)} %constant.58.clone.1, bf16[64,512]{1,0:T(8,128)(2,1)} %collective-permute-done.12), kind=kCustom, calls=%fused_computation.65 | custom fusion | flops 65536 | bytes 590336 | tf_op jit(solution)/shard_map/scatter-add | solution.py:120
  79.2 1.5 %scatter_custom_fusion.3 = f32[256,512]{1,0:T(8,128)S(1)} fusion(f32[256,512]{1,0:T(8,128)S(1)} %scatter_custom_fusion.2, s32[64]{0:T(128)} %copy-done.26, bf16[64,512]{1,0:T(8,128)(2,1)} %collective-permute-done.13), kind=kCustom, calls=%fused_computation.74 | custom fusion | flops 65536 | bytes 589824 | tf_op jit(solution)/shard_map/scatter-add | solution.py:120
  80.7 1.3 %scatter_custom_fusion.4 = f32[256,512]{1,0:T(8,128)S(1)} fusion(f32[256,512]{1,0:T(8,128)S(1)} %scatter_custom_fusion.3, s32[64]{0:T(128)} %copy-done.24, bf16[320,512]{1,0:T(8,128)(2,1)S(1)} %multiply_convert_fusion), kind=kCustom, calls=%fused_computation.72 | custom fusion | flops 65536 | bytes 589824 | tf_op jit(solution)/shard_map/scatter-add | solution.py:120
  82.1 1.6 %scatter_custom_fusion.5 = f32[256,512]{1,0:T(8,128)S(1)} fusion(f32[256,512]{1,0:T(8,128)S(1)} %scatter_custom_fusion.4, s32[64]{0:T(128)} %copy-done.27, bf16[64,512]{1,0:T(8,128)(2,1)} %collective-permute-done.14), kind=kCustom, calls=%fused_computation.70 | custom fusion | flops 65536 | bytes 589824 | tf_op jit(solution)/shard_map/scatter-add | solution.py:120
  83.7 1.5 %scatter_custom_fusion.6 = f32[256,512]{1,0:T(8,128)S(1)} fusion(f32[256,512]{1,0:T(8,128)S(1)} %scatter_custom_fusion.5, s32[64]{0:T(128)} %copy-done.25, bf16[64,512]{1,0:T(8,128)(2,1)S(1)} %collective-permute-done.15), kind=kCustom, calls=%fused_computation.68 | custom fusion | flops 65536 | bytes 589824 | tf_op jit(solution)/shard_map/scatter-add | solution.py:120
  85.2 0.3 fusion.26
  85.6 0.4 fusion.1
  86.0 0.4 copy-done.3
  86.4 0.4 copy-done.10
  86.7 0.5 fusion.70
  87.2 2.1 %copy.24 = f32[8,128,512]{2,0,1:T(8,128)} copy(f32[8,128,512]{1,2,0:T(8,128)S(1)} %bitcast.79) | data formatting | bytes 4194304 | tf_op jit(solution)/shard_map/reshape | solution.py:137
  89.3 3.5 %fusion.67 = (bf16[10,128,512]{2,0,1:T(8,128)(2,1)S(1)}, f32[10,128,512]{2,0,1:T(8,128)S(1)}) fusion(f32[8,128,512]{2,0,1:T(8,128)} %copy.24, s32[8]{0:T(128)S(1)} %eq.19), kind=kOutput, calls=%fused_computation.135 | convolution fusion | flops 63570000 | bytes 6029344 | tf_op jit(solution)/shard_map/wm,mjd->wjd/dot_general | solution.py:134
  92.8 0.7 fusion.65
  93.7 0.1 collective-permute-start.17
  93.8 0.4 collective-permute-start.18
  94.3 4.7 %collective-permute-start.16 = (bf16[256,512]{1,0:T(8,128)(2,1)S(1)}, bf16[256,512]{1,0:T(8,128)(2,1)S(1)}, u32[]{:S(2)}, u32[]{:S(2)}) collective-permute-start(bf16[256,512]{1,0:T(8,128)(2,1)S(1)} %bitcast.84), channel_id=1, source_target_pairs={{2,0},{3,1},{4,2},{5,3},{6,4},{7,5},{8,6},{9,7},{10,8},{11,9},{12,... | collective-permute-start | bytes 786440 | tf_op jit(solution)/shard_map/ppermute | solution.py:12
  99.0 1.0 fusion.3
  100.0 0.3 slice.100
  100.4 0.5 copy-done.12
  100.9 0.3 fusion.69
  101.3 2.9 %collective-permute-done.18 = bf16[256,512]{1,0:T(8,128)(2,1)S(1)} collective-permute-done((bf16[256,512]{1,0:T(8,128)(2,1)S(1)}, bf16[256,512]{1,0:T(8,128)(2,1)S(1)}, u32[]{:S(2)}, u32[]{:S(2)}) %collective-permute-start.18) | collective-permute-done | bytes 262176 | tf_op jit(solution)/shard_map/ppermute | solution.py:12
  104.2 2.3 %collective-permute-done.19 = bf16[256,512]{1,0:T(8,128)(2,1)S(1)} collective-permute-done((bf16[256,512]{1,0:T(8,128)(2,1)S(1)}, bf16[256,512]{1,0:T(8,128)(2,1)S(1)}, u32[]{:S(2)}, u32[]{:S(2)}) %collective-permute-start.19) | collective-permute-done | bytes 262176 | tf_op jit(solution)/shard_map/ppermute | solution.py:12
  106.5 5.7 %collective-permute-done.16 = bf16[256,512]{1,0:T(8,128)(2,1)S(1)} collective-permute-done((bf16[256,512]{1,0:T(8,128)(2,1)S(1)}, bf16[256,512]{1,0:T(8,128)(2,1)S(1)}, u32[]{:S(2)}, u32[]{:S(2)}) %collective-permute-start.16) | collective-permute-done | bytes 262176 | tf_op jit(solution)/shard_map/ppermute | solution.py:12
  112.3 0.2 fusion.22
  112.5 0.4 fusion.13
  112.9 0.6 copy-done.4
  113.5 0.9 fusion.17
  (111 shorter events, 1.5 us)
Async XLA Ops:
  0.6 1.3 %copy-start = (bf16[512,512]{1,0:T(8,128)(2,1)S(1)}, bf16[512,512]{1,0:T(8,128)(2,1)}, u32[]{:S(2)}) copy-start(bf16[512,512]{1,0:T(8,128)(2,1)} %param.17) | copy-start | bytes 1572868
  0.6 9.9 %copy-start.22 = (s32[1,5,64]{2,0,1:T(1,128)S(1)}, s32[1,5,64]{2,0,1:T(1,128)}, u32[]{:S(2)}) copy-start(s32[1,5,64]{2,0,1:T(1,128)} %param.25) | copy-start | bytes 3844
  0.7 9.9 %copy-start.21 = (s32[32,4]{0,1:T(4,128)S(1)}, s32[32,4]{0,1:T(4,128)}, u32[]{:S(2)}) copy-start(s32[32,4]{0,1:T(4,128)} %param.24) | copy-start | bytes 1540
  0.7 10.2 %copy-start.20 = (s32[1,5,64]{2,0,1:T(1,128)S(1)}, s32[1,5,64]{2,0,1:T(1,128)}, u32[]{:S(2)}) copy-start(s32[1,5,64]{2,0,1:T(1,128)} %param.26) | copy-start | bytes 3844
  0.7 10.3 %copy-start.23 = (s32[1,5]{1,0:T(1,128)S(1)}, s32[1,5]{1,0:T(1,128)}, u32[]{:S(2)}) copy-start(s32[1,5]{1,0:T(1,128)} %param.27) | copy-start | bytes 64
  0.7 10.4 %copy-start.7 = (bf16[512,512]{1,0:T(8,128)(2,1)S(1)}, bf16[512,512]{1,0:T(8,128)(2,1)}, u32[]{:S(2)}) copy-start(bf16[512,512]{1,0:T(8,128)(2,1)} %param.22) | copy-start | bytes 1572868
  0.7 10.4 %copy-start.18 = (bf16[128,512]{1,0:T(8,128)(2,1)S(1)}, bf16[128,512]{1,0:T(8,128)(2,1)}, u32[]{:S(2)}) copy-start(bf16[128,512]{1,0:T(8,128)(2,1)} %param.16) | copy-start | bytes 393220
  0.7 10.7 %copy-start.5 = (bf16[512,512]{1,0:T(8,128)(2,1)S(1)}, bf16[512,512]{1,0:T(8,128)(2,1)}, u32[]{:S(2)}) copy-start(bf16[512,512]{1,0:T(8,128)(2,1)} %param.21) | copy-start | bytes 1572868
  0.7 10.7 %copy-start.17 = (bf16[128,512]{1,0:T(8,128)(2,1)S(1)}, bf16[128,512]{1,0:T(8,128)(2,1)}, u32[]{:S(2)}) copy-start(bf16[128,512]{1,0:T(8,128)(2,1)} %param.15) | copy-start | bytes 393220
  3.2 39.6 %collective-permute-start.3 = (bf16[256,512]{1,0:T(8,128)(2,1)S(1)}, bf16[256,512]{1,0:T(8,128)(2,1)S(1)}, u32[]{:S(2)}, u32[]{:S(2)}) collective-permute-start(bf16[256,512]{1,0:T(8,128)(2,1)S(1)} %convolution_convert_fusion.1), channel_id=1, source_target_pairs={{2,0},{3,1},{4,2},{5,3},{6,4},{7,5},{8,6},{9,7},{10,8},{11,9},{12,... | collective-permute-start | bytes 786440 | tf_op jit(solution)/shard_map/ppermute | solution.py:12
  9.3 33.5 %collective-permute-start.2 = (bf16[256,512]{1,0:T(8,128)(2,1)S(1)}, bf16[256,512]{1,0:T(8,128)(2,1)S(1)}, u32[]{:S(2)}, u32[]{:S(2)}) collective-permute-start(bf16[256,512]{1,0:T(8,128)(2,1)S(1)} %convolution_convert_fusion.1), channel_id=1, source_target_pairs={{1,0},{2,1},{3,2},{4,3},{5,4},{6,5},{7,6},{8,7},{9,8},{10,9},{11,1... | collective-permute-start | bytes 786440 | tf_op jit(solution)/shard_map/ppermute | solution.py:12
  9.3 33.4 %collective-permute-start.1 = (bf16[256,512]{1,0:T(8,128)(2,1)S(1)}, bf16[256,512]{1,0:T(8,128)(2,1)S(1)}, u32[]{:S(2)}, u32[]{:S(2)}) collective-permute-start(bf16[256,512]{1,0:T(8,128)(2,1)S(1)} %convolution_convert_fusion.1), channel_id=1, source_target_pairs={{15,0},{0,1},{1,2},{2,3},{3,4},{4,5},{5,6},{6,7},{7,8},{8,9},{9,10... | collective-permute-start | bytes 786440 | tf_op jit(solution)/shard_map/ppermute | solution.py:12
  9.8 31.9 %collective-permute-start = (bf16[256,512]{1,0:T(8,128)(2,1)S(1)}, bf16[256,512]{1,0:T(8,128)(2,1)}, u32[]{:S(2)}, u32[]{:S(2)}) collective-permute-start(bf16[256,512]{1,0:T(8,128)(2,1)S(1)} %convolution_convert_fusion.1), channel_id=1, source_target_pairs={{14,0},{15,1},{0,2},{1,3},{2,4},{3,5},{4,6},{5,7},{6,8},{7,9},{8,1... | collective-permute-start | bytes 786440 | tf_op jit(solution)/shard_map/ppermute | solution.py:12
  10.5 11.4 %collective-permute-start.10 = (s32[64]{0:T(128)S(1)}, s32[64]{0:T(128)S(1)}, u32[]{:S(2)}, u32[]{:S(2)}) collective-permute-start(s32[64]{0:T(128)S(1)} %get-tuple-element.13), channel_id=1, source_target_pairs={{14,0},{15,1},{0,2},{1,3},{2,4},{3,5},{4,6},{5,7},{6,8},{7,9},{8,1... | collective-permute-start | bytes 776 | tf_op jit(solution)/shard_map/ppermute | solution.py:12
  10.6 1.3 %copy-start.24 = (s32[64]{0:T(128)}, s32[64]{0:T(128)S(1)}, u32[]{:S(2)}) copy-start(s32[64]{0:T(128)S(1)} %fusion.61) | copy-start | bytes 772
  21.9 9.1 %collective-permute-start.6 = (s32[64]{0:T(128)S(1)}, s32[64]{0:T(128)S(1)}, u32[]{:S(2)}, u32[]{:S(2)}) collective-permute-start(s32[64]{0:T(128)S(1)} %get-tuple-element.14), channel_id=1, source_target_pairs={{1,0},{2,1},{3,2},{4,3},{5,4},{6,5},{7,6},{8,7},{9,8},{10,9},{11,1... | collective-permute-start | bytes 776 | tf_op jit(solution)/shard_map/ppermute | solution.py:12
  29.8 21.2 %copy-start.25 = (s32[64]{0:T(128)}, s32[64]{0:T(128)S(1)}, u32[]{:S(2)}) copy-start(s32[64]{0:T(128)S(1)} %compare_select_fusion.3) | copy-start | bytes 772
  31.1 3.5 %collective-permute-start.4 = (s32[64]{0:T(128)S(1)}, s32[64]{0:T(128)S(1)}, u32[]{:S(2)}, u32[]{:S(2)}) collective-permute-start(s32[64]{0:T(128)S(1)} %get-tuple-element.15), channel_id=1, source_target_pairs={{2,0},{3,1},{4,2},{5,3},{6,4},{7,5},{8,6},{9,7},{10,8},{11,9},{12,... | collective-permute-start | bytes 776 | tf_op jit(solution)/shard_map/ppermute | solution.py:12
  31.1 11.8 %copy-start.26 = (s32[64]{0:T(128)}, s32[64]{0:T(128)S(1)}, u32[]{:S(2)}) copy-start(s32[64]{0:T(128)S(1)} %compare_select_fusion.6) | copy-start | bytes 772
  34.6 7.1 %collective-permute-start.8 = (s32[64]{0:T(128)S(1)}, s32[64]{0:T(128)S(1)}, u32[]{:S(2)}, u32[]{:S(2)}) collective-permute-start(s32[64]{0:T(128)S(1)} %get-tuple-element.16), channel_id=1, source_target_pairs={{15,0},{0,1},{1,2},{2,3},{3,4},{4,5},{5,6},{6,7},{7,8},{8,9},{9,10... | collective-permute-start | bytes 776 | tf_op jit(solution)/shard_map/ppermute | solution.py:12
  36.3 6.6 %copy-start.28 = (s32[64]{0:T(128)}, s32[64]{0:T(128)S(1)}, u32[]{:S(2)}) copy-start(s32[64]{0:T(128)S(1)} %compare_select_fusion.7) | copy-start | bytes 772
  41.7 9.2 %copy-start.27 = (s32[64]{0:T(128)}, s32[64]{0:T(128)S(1)}, u32[]{:S(2)}) copy-start(s32[64]{0:T(128)S(1)} %compare_select_fusion.4) | copy-start | bytes 772
  42.9 1.1 copy-start.9
  45.9 1.4 %copy-start.1 = (bf16[256,512]{1,0:T(8,128)(2,1)S(1)}, bf16[256,512]{1,0:T(8,128)(2,1)}, u32[]{:S(2)}) copy-start(bf16[256,512]{1,0:T(8,128)(2,1)} %param.14) | copy-start | bytes 786436
  45.9 1.4 %copy-start.2 = (bf16[512,512]{1,0:T(8,128)(2,1)S(1)}, bf16[512,512]{1,0:T(8,128)(2,1)}, u32[]{:S(2)}) copy-start(bf16[512,512]{1,0:T(8,128)(2,1)} %param.18) | copy-start | bytes 1572868
  47.3 1.2 %copy-start.14 = (bf16[512,512]{1,0:T(8,128)(2,1)S(1)}, bf16[512,512]{1,0:T(8,128)(2,1)}, u32[]{:S(2)}) copy-start(bf16[512,512]{1,0:T(8,128)(2,1)} %param.20) | copy-start | bytes 1572868
  50.9 9.4 %collective-permute-start.5 = (bf16[64,512]{1,0:T(8,128)(2,1)S(1)}, bf16[64,512]{1,0:T(8,128)(2,1)S(1)}, u32[]{:S(2)}, u32[]{:S(2)}) collective-permute-start(bf16[64,512]{1,0:T(8,128)(2,1)S(1)} %gather_fusion.1), channel_id=1, source_target_pairs={{14,0},{15,1},{0,2},{1,3},{2,4},{3,5},{4,6},{5,7},{6,8},{7,9},{8,1... | collective-permute-start | bytes 196616 | tf_op jit(solution)/shard_map/ppermute | solution.py:12
  53.8 6.5 %collective-permute-start.7 = (bf16[64,512]{1,0:T(8,128)(2,1)S(1)}, bf16[64,512]{1,0:T(8,128)(2,1)S(1)}, u32[]{:S(2)}, u32[]{:S(2)}) collective-permute-start(bf16[64,512]{1,0:T(8,128)(2,1)S(1)} %gather_fusion.2), channel_id=1, source_target_pairs={{15,0},{0,1},{1,2},{2,3},{3,4},{4,5},{5,6},{6,7},{7,8},{8,9},{9,10... | collective-permute-start | bytes 196616 | tf_op jit(solution)/shard_map/ppermute | solution.py:12
  53.8 6.8 %collective-permute-start.9 = (bf16[64,512]{1,0:T(8,128)(2,1)S(1)}, bf16[64,512]{1,0:T(8,128)(2,1)S(1)}, u32[]{:S(2)}, u32[]{:S(2)}) collective-permute-start(bf16[64,512]{1,0:T(8,128)(2,1)S(1)} %gather_fusion.4), channel_id=1, source_target_pairs={{1,0},{2,1},{3,2},{4,3},{5,4},{6,5},{7,6},{8,7},{9,8},{10,9},{11,1... | collective-permute-start | bytes 196616 | tf_op jit(solution)/shard_map/ppermute | solution.py:12
  58.3 4.3 %collective-permute-start.11 = (bf16[64,512]{1,0:T(8,128)(2,1)S(1)}, bf16[64,512]{1,0:T(8,128)(2,1)S(1)}, u32[]{:S(2)}, u32[]{:S(2)}) collective-permute-start(bf16[64,512]{1,0:T(8,128)(2,1)S(1)} %gather_fusion.5), channel_id=1, source_target_pairs={{2,0},{3,1},{4,2},{5,3},{6,4},{7,5},{8,6},{9,7},{10,8},{11,9},{12,... | collective-permute-start | bytes 196616 | tf_op jit(solution)/shard_map/ppermute | solution.py:12
  62.5 10.2 %copy-start.8 = (bf16[512,512]{1,0:T(8,128)(2,1)S(1)}, bf16[512,512]{1,0:T(8,128)(2,1)}, u32[]{:S(2)}) copy-start(bf16[512,512]{1,0:T(8,128)(2,1)} %param.22) | copy-start | bytes 1572868
  63.5 20.2 %collective-permute-start.15 = (bf16[64,512]{1,0:T(8,128)(2,1)}, bf16[64,512]{1,0:T(8,128)(2,1)S(1)}, u32[]{:S(2)}, u32[]{:S(2)}) collective-permute-start(bf16[64,512]{1,0:T(8,128)(2,1)} %get-tuple-element.9), channel_id=1, source_target_pairs={{14,0},{15,1},{0,2},{1,3},{2,4},{3,5},{4,6},{5,7},{6,8},{7,9},{8,1... | collective-permute-start | bytes 196616 | tf_op jit(solution)/shard_map/ppermute | solution.py:12
  63.5 18.5 %collective-permute-start.14 = (bf16[64,512]{1,0:T(8,128)(2,1)}, bf16[64,512]{1,0:T(8,128)(2,1)}, u32[]{:S(2)}, u32[]{:S(2)}) collective-permute-start(bf16[64,512]{1,0:T(8,128)(2,1)} %get-tuple-element.10), channel_id=1, source_target_pairs={{15,0},{0,1},{1,2},{2,3},{3,4},{4,5},{5,6},{6,7},{7,8},{8,9},{9,10... | collective-permute-start | bytes 196616 | tf_op jit(solution)/shard_map/ppermute | solution.py:12
  63.5 15.6 %collective-permute-start.13 = (bf16[64,512]{1,0:T(8,128)(2,1)}, bf16[64,512]{1,0:T(8,128)(2,1)}, u32[]{:S(2)}, u32[]{:S(2)}) collective-permute-start(bf16[64,512]{1,0:T(8,128)(2,1)} %get-tuple-element.11), channel_id=1, source_target_pairs={{1,0},{2,1},{3,2},{4,3},{5,4},{6,5},{7,6},{8,7},{9,8},{10,9},{11,1... | collective-permute-start | bytes 196616 | tf_op jit(solution)/shard_map/ppermute | solution.py:12
  68.0 9.7 %collective-permute-start.12 = (bf16[64,512]{1,0:T(8,128)(2,1)S(1)}, bf16[64,512]{1,0:T(8,128)(2,1)}, u32[]{:S(2)}, u32[]{:S(2)}) collective-permute-start(bf16[64,512]{1,0:T(8,128)(2,1)S(1)} %get-tuple-element.12), channel_id=1, source_target_pairs={{2,0},{3,1},{4,2},{5,3},{6,4},{7,5},{8,6},{9,7},{10,8},{11,9},{12,... | collective-permute-start | bytes 196616 | tf_op jit(solution)/shard_map/ppermute | solution.py:12
  79.2 6.1 %copy-start.15 = (bf16[512,512]{1,0:T(8,128)(2,1)S(1)}, bf16[512,512]{1,0:T(8,128)(2,1)}, u32[]{:S(2)}) copy-start(bf16[512,512]{1,0:T(8,128)(2,1)} %param.20) | copy-start | bytes 1572868
  82.1 3.5 %copy-start.16 = (f32[256,512]{1,0:T(8,128)S(1)}, f32[256,512]{1,0:T(8,128)}, u32[]{:S(2)}) copy-start(f32[256,512]{1,0:T(8,128)} %convolution_add_fusion.2) | copy-start | bytes 1572868
  82.1 3.5 %copy-start.29 = (bf16[512,512]{1,0:T(8,128)(2,1)S(1)}, bf16[512,512]{1,0:T(8,128)(2,1)}, u32[]{:S(2)}) copy-start(bf16[512,512]{1,0:T(8,128)(2,1)} %param.19) | copy-start | bytes 1572868
  85.6 0.8 copy-start.3
  85.6 1.1 copy-start.10
  86.4 0.8 copy-start.11
  93.5 5.5 %copy-start.6 = (bf16[512,512]{1,0:T(8,128)(2,1)S(1)}, bf16[512,512]{1,0:T(8,128)(2,1)}, u32[]{:S(2)}) copy-start(bf16[512,512]{1,0:T(8,128)(2,1)} %param.21) | copy-start | bytes 1572868
  93.5 5.5 %copy-start.13 = (f32[128,512]{1,0:T(8,128)S(1)}, f32[128,512]{1,0:T(8,128)}, u32[]{:S(2)}) copy-start(f32[128,512]{1,0:T(8,128)} %scatter_custom_fusion.1) | copy-start | bytes 786436
  93.5 5.5 %copy-start.19 = (bf16[128,512]{1,0:T(8,128)(2,1)S(1)}, bf16[128,512]{1,0:T(8,128)(2,1)}, u32[]{:S(2)}) copy-start(bf16[128,512]{1,0:T(8,128)(2,1)} %param.16) | copy-start | bytes 393220
  93.7 7.5 %collective-permute-start.17 = (bf16[256,512]{1,0:T(8,128)(2,1)S(1)}, bf16[256,512]{1,0:T(8,128)(2,1)S(1)}, u32[]{:S(2)}, u32[]{:S(2)}) collective-permute-start(bf16[256,512]{1,0:T(8,128)(2,1)S(1)} %bitcast.87), channel_id=1, source_target_pairs={{1,0},{2,1},{3,2},{4,3},{5,4},{6,5},{7,6},{8,7},{9,8},{10,9},{11,1... | collective-permute-start | bytes 786440 | tf_op jit(solution)/shard_map/ppermute | solution.py:12
  93.8 10.4 %collective-permute-start.18 = (bf16[256,512]{1,0:T(8,128)(2,1)S(1)}, bf16[256,512]{1,0:T(8,128)(2,1)S(1)}, u32[]{:S(2)}, u32[]{:S(2)}) collective-permute-start(bf16[256,512]{1,0:T(8,128)(2,1)S(1)} %bitcast.86), channel_id=1, source_target_pairs={{15,0},{0,1},{1,2},{2,3},{3,4},{4,5},{5,6},{6,7},{7,8},{8,9},{9,10... | collective-permute-start | bytes 786440 | tf_op jit(solution)/shard_map/ppermute | solution.py:12
  94.3 12.3 %collective-permute-start.19 = (bf16[256,512]{1,0:T(8,128)(2,1)S(1)}, bf16[256,512]{1,0:T(8,128)(2,1)S(1)}, u32[]{:S(2)}, u32[]{:S(2)}) collective-permute-start(bf16[256,512]{1,0:T(8,128)(2,1)S(1)} %bitcast.85), channel_id=1, source_target_pairs={{14,0},{15,1},{0,2},{1,3},{2,4},{3,5},{4,6},{5,7},{6,8},{7,9},{8,1... | collective-permute-start | bytes 786440 | tf_op jit(solution)/shard_map/ppermute | solution.py:12
  94.3 18.0 %collective-permute-start.16 = (bf16[256,512]{1,0:T(8,128)(2,1)S(1)}, bf16[256,512]{1,0:T(8,128)(2,1)S(1)}, u32[]{:S(2)}, u32[]{:S(2)}) collective-permute-start(bf16[256,512]{1,0:T(8,128)(2,1)S(1)} %bitcast.84), channel_id=1, source_target_pairs={{2,0},{3,1},{4,2},{5,3},{6,4},{7,5},{8,6},{9,7},{10,8},{11,9},{12,... | collective-permute-start | bytes 786440 | tf_op jit(solution)/shard_map/ppermute | solution.py:12
  100.0 0.9 copy-start.12
  112.5 1.0 copy-start.4
where the time goes:
time: 115 us; the launch traced here: 114 us
  starting transfers between devices  35.1 us (31%)
  waiting for transfers between devices  29.8 us (26%)
  local copies, waits for them, and re-layouts  17.7 us (15%)
  other arithmetic  16.1 us (14%)
  matrix products  14.3 us (12%)
  between operations  1.35 us (1%)
    ppermute x20, starting transfers between devices, passed_along(): return lax.ppermute(block, axis, route)  35.1 us
    ppermute x20, waiting for transfers between devices, passed_along(): return lax.ppermute(block, axis, route)  29.8 us
    scatter-add x5, other arithmetic, body(): d_src_total = d_src_total.at[held[place]].add(back.astype(jnp.float32))  7.36 us
    unnamed x68, local copies, waits for them, and re-layouts  4.13 us
    dot_general x1, matrix products, body(): jnp.einsum('wm,mjd->wjd', spots, contrib.reshape(blocks * neighbours, 128...  3.53 us
    gather x5, local copies, waits for them, and re-layouts, body(): rows_out = src_proj[held[place]]  3.51 us
    scatter-add x1, other arithmetic, body(): d_dst = jnp.zeros((grid_rows, width), jnp.float32).at[dst].add(d_edge.ast...  3.17 us
    scatter-add x1, other arithmetic, body(): jnp.zeros((grid_rows, width), jnp.float32).at[dst].add(edge)  2.74 us
  transfers between devices with their start and end apart: 20, of which 9 were waited for; matrix products, arithmetic and copies ran while one was open for 21% of the time, Pallas kernels for 0%

commit v1 on v0

v1 whole, which is shorter than its diff:
```python
import functools

import jax
import jax.numpy as jnp
from jax import lax
from jax.experimental import pallas as pl
from jax.experimental.pallas import tpu as pltpu
from jax.sharding import PartitionSpec as P

REACH = 2
CHUNKS = 4
EDGE_CHUNKS = 2
F32 = jnp.float32
BF16 = jnp.bfloat16


def mm(a, b):
    return jnp.dot(a, b, preferred_element_type=F32)


def mm_nt(a, b):
    return lax.dot_general(a, b, (((1,), (1,)), ((), ())), preferred_element_type=F32)


def silu_grad(value, sig):
    return sig * (1.0 + value * (1.0 - sig))


def kernel(
    n,
    mesh_hbm,
    grid_hbm,
    cot_hbm,
    w_send_hbm,
    w_self_hbm,
    w_out_hbm,
    w_src_hbm,
    w_dst_hbm,
    w_dec_hbm,
    adj_hbm,
    adj_index,
    idx,
    grid_out_hbm,
    grad_grid_hbm,
    grad_mesh_hbm,
    mesh,
    grid,
    cot,
    w_send,
    w_self,
    w_out,
    w_src,
    w_dst,
    w_dec,
    adj,
    nb,
    pre,
    win,
    dense,
    back_dense,
    held,
    pick,
    pick_t,
    join,
    join_t,
    dproj,
    dsum,
    mesh_out,
    rows_out,
    rows_in,
    edge,
    d_edge,
    back,
    sgrad,
    d_mesh,
    d_pre,
    g_own,
    g_two,
    g_three,
    k_out,
    k_in,
    z_out,
    z_in,
    y_out,
    y_in,
    res_a,
    res_b,
    res_c,
    load_sem,
    store_sem,
    idx_send,
    idx_recv,
    win_send,
    win_recv,
    row_send,
    row_recv,
    back_send,
    back_recv,
    k_send,
    k_recv,
    z_send,
    z_recv,
    y_send,
    y_recv,
):
    per_dev, width = mesh.shape
    grid_rows = grid.shape[0]
    blocks, neighbours = adj.shape[0], adj.shape[1]
    cw = width // CHUNKS
    ew = width // EDGE_CHUNKS
    me = lax.axis_index("blk")
    core = lax.rem(me, 2)
    odd = lax.rem(me // 2, 2)
    side = 1 - 2 * odd

    def at(offset):
        return {"blk": lax.rem(me + offset + n, n)}

    mate = at(1 - 2 * core)
    y_mate = at(2 * side)
    ahead = at(4 * side)
    behind = at(-4 * side)
    turn = lax.rem(core + odd, 2)
    passed = 2 + turn
    turn32 = turn.astype(F32)

    barrier = pltpu.get_barrier_semaphore()
    for offset in (-4, -2, -1, 1, 2, 4):
        pl.semaphore_signal(barrier, inc=1, device_id=at(offset), device_id_type=pl.DeviceIdType.MESH)

    pairs = [
        (mesh_hbm, mesh),
        (w_send_hbm, w_send),
        (adj_hbm, adj),
        (w_self_hbm, w_self),
        (grid_hbm, grid),
        (w_dst_hbm, w_dst),
        (cot_hbm, cot),
        (w_dec_hbm, w_dec),
        (w_out_hbm, w_out),
        (w_src_hbm, w_src),
    ]
    loads = [pltpu.make_async_copy(a, b, load_sem.at[i]) for i, (a, b) in enumerate(pairs)]
    for copy in loads:
        copy.start()

    def remote(src, dst, send, recv, device):
        return pltpu.make_async_remote_copy(
            src_ref=src,
            dst_ref=dst,
            send_sem=send,
            recv_sem=recv,
            device_id=device,
            device_id_type=pl.DeviceIdType.MESH,
        )

    loads[0].wait()
    h32 = mesh[...].astype(F32)
    scale = lax.rsqrt(jnp.mean(h32 * h32, axis=-1, keepdims=True) + 1e-05)
    nb[...] = (h32 * scale).astype(BF16)
    loads[1].wait()

    sends = []

    def panel(chunk, slot, dst_slot, number, device):
        copy = remote(
            win.at[chunk, slot],
            win.at[chunk, dst_slot],
            win_send.at[chunk, number],
            win_recv.at[chunk, dst_slot - 1],
            device,
        )
        copy.start()
        sends.append(copy)

    def arrived(chunk, slot):
        remote(
            win.at[chunk, slot], win.at[chunk, slot], win_send.at[chunk, 0], win_recv.at[chunk, slot - 1], mate
        ).wait_recv()

    for c in range(CHUNKS):
        win[c, 0] = mm(nb[...], w_send[:, c * cw : (c + 1) * cw]).astype(BF16)
        if c == 0:
            pl.semaphore_wait(barrier, 6)
        panel(c, 0, 2, 0, y_mate)
        panel(c, 0, 1, 1, mate)

    idx_copies = []
    for place in range(2 * REACH + 1):
        if place != REACH:
            copy = remote(
                idx.at[place], held.at[place], idx_send.at[place], idx_recv.at[place], at(place - REACH)
            )
            copy.start()
            idx_copies.append(copy)

    def hop_y(c):
        arrived(c, 2)
        panel(c, 2, 3, 2, ahead)

    def hop_core(c):
        arrived(c, 3)
        panel(c, passed, 4, 3, mate)

    loads[2].wait()
    for b in range(blocks):
        slots = []
        for k in range(neighbours):
            named = adj_index[me * blocks + b, k]
            away = lax.rem(named // blocks - me + n, n)
            away = jnp.where(away > REACH, away - n, away)
            slot = jnp.where(
                away == 0,
                0,
                jnp.where(
                    away == 1 - 2 * core,
                    1,
                    jnp.where(away == 2 * side, 2, jnp.where(away == -2 * side, 3, 4)),
                ),
            )
            slots.append(slot * blocks + lax.rem(named, blocks))
        for w in range((2 * REACH + 1) * blocks):
            total = jnp.zeros((128, 128), F32)
            for k in range(neighbours):
                total = total + adj[b, k].astype(F32) * (slots[k] == w).astype(F32)
            dense[b * 128 : (b + 1) * 128, w * 128 : (w + 1) * 128] = total.astype(BF16)
            back_dense[w * 128 : (w + 1) * 128, b * 128 : (b + 1) * 128] = total.astype(BF16)

    hop_y(0)
    loads[3].wait()
    pre[...] = mm(nb[...], w_self[...])
    hop_y(1)
    hop_core(0)

    lanes = lax.broadcasted_iota(jnp.int32, (128, 128), 1).astype(F32)
    subs = lax.broadcasted_iota(jnp.int32, (per_dev, 128), 0).astype(F32)
    for t in range(3):
        row = idx[5, t : t + 1, :].astype(F32)
        whole = jnp.broadcast_to(row, (128, 128))
        hot = (whole.T == lanes).astype(F32).astype(BF16)
        join[t * 128 : (t + 1) * 128, 0:128] = hot
        join[t * 128 : (t + 1) * 128, 128:256] = hot
        join_t[:, t * 128 : (t + 1) * 128] = (whole == subs[:128]).astype(F32).astype(BF16)

    loads[4].wait()
    loads[5].wait()
    proj = mm(grid[...], w_dst[...])
    high = proj.astype(BF16)
    low = (proj - high.astype(F32)).astype(BF16)
    dproj[...] = mm(join[...], jnp.concatenate([high, low], axis=0))
    if CHUNKS > 2:
        hop_y(2)
        hop_core(1)
    loads[6].wait()
    loads[7].wait()
    dsum[...] = mm(join[:, 0:128], mm_nt(cot[...], w_dec[...]).astype(BF16)).astype(BF16)

    for copy in idx_copies:
        copy.wait()
    half = lax.broadcasted_iota(jnp.int32, (1, 128), 1) < 64
    index_rows = []
    for place in range(6):
        if place == REACH:
            index_rows.append(idx[place, 0:1, :])
        elif place == 5:
            index_rows.append(jnp.full((1, 128), -1, jnp.int32))
        else:
            index_rows.append(held[place, 0:1, :])
    for t in range(3):
        row = jnp.where(half, index_rows[2 * t], index_rows[2 * t + 1]).astype(F32)
        whole = jnp.broadcast_to(row, (128, 128))
        turned = whole.T
        for u in range(per_dev // 128):
            pick[t * 128 : (t + 1) * 128, u * 128 : (u + 1) * 128] = (
                (turned == lanes + float(u * 128)).astype(F32).astype(BF16)
            )
        pick_t[:, t * 128 : (t + 1) * 128] = (jnp.broadcast_to(row, (per_dev, 128)) == subs).astype(F32).astype(BF16)
    live = 320
    for e in range(EDGE_CHUNKS):
        edge[e, live:384] = jnp.zeros((64, ew), BF16)
        d_edge[e, live:384] = jnp.zeros((64, ew), BF16)
        back[e, live:384] = jnp.zeros((64, ew), BF16)
    loads[8].wait()
    loads[9].wait()

    def mesh_chunk(c, acc):
        arrived(c, 1)
        arrived(c, 4)
        cols = slice(c * cw, (c + 1) * cw)
        value = pre[:, cols] + mm(dense[...], win[c].reshape(5 * per_dev, cw))
        pre[:, cols] = value
        act = (value * jax.nn.sigmoid(value)).astype(BF16)
        return acc + mm(act, w_out[cols, :])

    acc = mesh[...].astype(F32)
    done_y = min(3, CHUNKS) if CHUNKS > 2 else 2
    done_core = done_y - 1
    for c in range(CHUNKS):
        if done_y < CHUNKS:
            hop_y(done_y)
            done_y += 1
        if done_core < CHUNKS:
            hop_core(done_core)
            done_core += 1
        acc = mesh_chunk(c, acc)
    mesh_out[...] = acc.astype(BF16)

    order = (0, 4, 1, 3)
    for e in range(EDGE_CHUNKS):
        cols = slice(e * ew, (e + 1) * ew)
        src = mm(mesh_out[...], w_src[:, cols]).astype(BF16)
        rows_out[e] = mm(pick[...], src).astype(BF16)
        for place in order:
            rows = pl.ds(place * 64, 64)
            copy = remote(
                rows_out.at[e, rows],
                rows_in.at[e, rows],
                row_send.at[e, place],
                row_recv.at[e, place],
                at(REACH - place),
            )
            copy.start()
            sends.append(copy)

    value = pre[...]
    sgrad[...] = silu_grad(value, jax.nn.sigmoid(value))

    for e in range(EDGE_CHUNKS):
        cols = slice(e * ew, (e + 1) * ew)
        for place in (2, 3, 1, 4, 0):
            rows = slice(place * 64, (place + 1) * 64)
            span = pl.ds(place * 64, 64)
            if place == REACH:
                got = rows_out[e, rows]
            else:
                remote(
                    rows_in.at[e, span], rows_in.at[e, span], row_send.at[e, place], row_recv.at[e, place], mate
                ).wait_recv()
                got = rows_in[e, rows]
            joined = got.astype(F32) + dproj[rows, cols]
            sig = jax.nn.sigmoid(joined)
            edge[e, rows] = (joined * sig).astype(BF16)
            grad = (dsum[rows, cols].astype(F32) * silu_grad(joined, sig)).astype(BF16)
            d_edge[e, rows] = grad
            if place == REACH:
                back[e, rows] = grad
            else:
                copy = remote(
                    d_edge.at[e, span],
                    back.at[e, span],
                    back_send.at[e, place],
                    back_recv.at[e, place],
                    at(place - REACH),
                )
                copy.start()
                sends.append(copy)

    out_acc = grid[...].astype(F32)
    grad_acc = cot[...].astype(F32)
    for e in range(EDGE_CHUNKS):
        cols = slice(e * ew, (e + 1) * ew)
        out_acc += mm(mm(join_t[...], edge[e]).astype(BF16), w_dec[cols, :])
        grad_acc += mm_nt(mm(join_t[...], d_edge[e]).astype(BF16), w_dst[:, cols])
    res_a[...] = out_acc.astype(BF16)
    res_b[...] = grad_acc.astype(BF16)
    out_a = pltpu.make_async_copy(res_a, grid_out_hbm, store_sem.at[0])
    out_b = pltpu.make_async_copy(res_b, grad_grid_hbm, store_sem.at[1])
    out_a.start()
    out_b.start()

    acc = jnp.zeros((per_dev, width), F32)
    for e in range(EDGE_CHUNKS):
        cols = slice(e * ew, (e + 1) * ew)
        for place in (3, 1, 4, 0):
            span = pl.ds(place * 64, 64)
            remote(
                back.at[e, span], back.at[e, span], back_send.at[e, place], back_recv.at[e, place], mate
            ).wait_recv()
        acc += mm_nt(mm(pick_t[...], back[e]).astype(BF16), w_src[:, cols])
    d_mesh[...] = acc
    mesh_out[...] = acc.astype(BF16)

    def spread(c):
        cols = slice(c * cw, (c + 1) * cw)
        slope = (mm_nt(mesh_out[...], w_out[cols, :]) * sgrad[:, cols]).astype(BF16)
        d_pre[:, cols] = slope

        def product(slot):
            return mm(back_dense[slot * per_dev : (slot + 1) * per_dev, :], slope)

        k_out[c, 1] = product(4).astype(BF16)
        copy = remote(k_out.at[c, 1], k_in.at[c, 1], k_send.at[c, 1], k_recv.at[c, 1], mate)
        copy.start()
        sends.append(copy)
        k_out[c, 0] = product(1).astype(BF16)
        copy = remote(k_out.at[c, 0], k_in.at[c, 0], k_send.at[c, 0], k_recv.at[c, 0], mate)
        copy.start()
        sends.append(copy)
        g_three[c] = product(3)
        g_two[c] = product(2)
        g_own[c] = product(0)

    def fold_core(c):
        remote(k_out.at[c, 1], k_in.at[c, 1], k_send.at[c, 1], k_recv.at[c, 1], mate).wait_recv()
        came = k_in[c, 1].astype(F32)
        z_out[c] = (g_three[c] + came * turn32).astype(BF16)
        copy = remote(z_out.at[c], z_in.at[c], z_send.at[c], z_recv.at[c], behind)
        copy.start()
        sends.append(copy)
        g_two[c] = g_two[c] + came * (1.0 - turn32)

    def fold_z(c):
        remote(z_out.at[c], z_in.at[c], z_send.at[c], z_recv.at[c], behind).wait_recv()
        y_out[c] = (g_two[c] + z_in[c].astype(F32)).astype(BF16)
        copy = remote(y_out.at[c], y_in.at[c], y_send.at[c], y_recv.at[c], y_mate)
        copy.start()
        sends.append(copy)

    def fold_y(c):
        remote(k_out.at[c, 0], k_in.at[c, 0], k_send.at[c, 0], k_recv.at[c, 0], mate).wait_recv()
        remote(y_out.at[c], y_in.at[c], y_send.at[c], y_recv.at[c], y_mate).wait_recv()
        total = g_own[c] + k_in[c, 0].astype(F32) + y_in[c].astype(F32)
        return mm_nt(total.astype(BF16), w_send[:, c * cw : (c + 1) * cw])

    acc = None
    for step in range(CHUNKS + 3):
        if step < CHUNKS:
            spread(step)
        if 0 <= step - 1 < CHUNKS:
            fold_core(step - 1)
        if 0 <= step - 2 < CHUNKS:
            fold_z(step - 2)
        if step == CHUNKS:
            acc = mm_nt(d_pre[...], w_self[...])
        if step == CHUNKS + 1:
            for c in range(CHUNKS - 2):
                acc += fold_y(c)
    for c in range(max(CHUNKS - 2, 0), CHUNKS):
        acc += fold_y(c)

    h32 = mesh[...].astype(F32)
    scale = lax.rsqrt(jnp.mean(h32 * h32, axis=-1, keepdims=True) + 1e-05)
    normed = h32 * scale
    res_c[...] = (
        d_mesh[...] + scale * (acc - normed * jnp.mean(acc * normed, axis=-1, keepdims=True))
    ).astype(BF16)
    out_c = pltpu.make_async_copy(res_c, grad_mesh_hbm, store_sem.at[2])
    out_c.start()
    for copy in sends:
        copy.wait_send()
    out_a.wait()
    out_b.wait()
    out_c.wait()


def body(
    mesh_in,
    grid_in,
    cotangent,
    w_send,
    w_self,
    w_out,
    w_src,
    w_dst,
    w_dec,
    adj_blocks,
    adj_index,
    src_rows,
    dst_rows,
    counts,
):
    n = lax.axis_size("blk")
    per_dev, width = mesh_in.shape
    grid_rows = grid_in.shape[0]
    places, slots = src_rows.shape[1], src_rows.shape[2]
    cw, ew = width // CHUNKS, width // EDGE_CHUNKS
    src = jnp.concatenate([src_rows[0], src_rows[0]], axis=-1)
    src = jnp.broadcast_to(src[:, None, :], (places, 8, 2 * slots))
    alive = jnp.arange(slots, dtype=jnp.int32)[None, :] < counts[0][:, None]
    dst = jnp.where(alive, dst_rows[0], -1)
    dst = jnp.pad(dst, ((0, 11), (0, 0)), constant_values=-1).reshape(1, 8, 2 * slots)
    idx = jnp.concatenate([src, dst], axis=0)

    def vmem(*shape, dtype=BF16):
        return pltpu.VMEM(shape, dtype)

    dma = pltpu.SemaphoreType.DMA
    weight = vmem(width, width)
    pad = 384
    scratch = [
        vmem(per_dev, width),
        vmem(grid_rows, width),
        vmem(grid_rows, width),
        weight,
        weight,
        weight,
        weight,
        weight,
        weight,
        vmem(*adj_blocks.shape),
        vmem(per_dev, width),
        vmem(per_dev, width, dtype=F32),
        vmem(CHUNKS, 5, per_dev, cw),
        vmem(per_dev, 5 * per_dev),
        vmem(5 * per_dev, per_dev),
        vmem(5, 8, 128, dtype=jnp.int32),
        vmem(pad, per_dev),
        vmem(per_dev, pad),
        vmem(pad, 2 * grid_rows),
        vmem(grid_rows, pad),
        vmem(pad, width, dtype=F32),
        vmem(pad, width),
        vmem(per_dev, width),
        vmem(EDGE_CHUNKS, pad, ew),
        vmem(EDGE_CHUNKS, pad, ew),
        vmem(EDGE_CHUNKS, pad, ew),
        vmem(EDGE_CHUNKS, pad, ew),
        vmem(EDGE_CHUNKS, pad, ew),
        vmem(per_dev, width, dtype=F32),
        vmem(per_dev, width, dtype=F32),
        vmem(per_dev, width),
        vmem(CHUNKS, per_dev, cw, dtype=F32),
        vmem(CHUNKS, per_dev, cw, dtype=F32),
        vmem(CHUNKS, per_dev, cw, dtype=F32),
        vmem(CHUNKS, 2, per_dev, cw),
        vmem(CHUNKS, 2, per_dev, cw),
        vmem(CHUNKS, per_dev, cw),
        vmem(CHUNKS, per_dev, cw),
        vmem(CHUNKS, per_dev, cw),
        vmem(CHUNKS, per_dev, cw),
        vmem(grid_rows, width),
        vmem(grid_rows, width),
        vmem(per_dev, width),
        dma((10,)),
        dma((3,)),
        dma((5,)),
        dma((5,)),
        dma((CHUNKS, 4)),
        dma((CHUNKS, 4)),
        dma((EDGE_CHUNKS, 5)),
        dma((EDGE_CHUNKS, 5)),
        dma((EDGE_CHUNKS, 5)),
        dma((EDGE_CHUNKS, 5)),
        dma((CHUNKS, 2)),
        dma((CHUNKS, 2)),
        dma((CHUNKS,)),
        dma((CHUNKS,)),
        dma((CHUNKS,)),
        dma((CHUNKS,)),
    ]
    hbm = pl.BlockSpec(memory_space=pl.ANY)
    return pl.pallas_call(
        functools.partial(kernel, n),
        out_shape=(
            jax.ShapeDtypeStruct(grid_in.shape, BF16),
            jax.ShapeDtypeStruct(grid_in.shape, BF16),
            jax.ShapeDtypeStruct(mesh_in.shape, BF16),
        ),
        in_specs=[hbm] * 10
        + [pl.BlockSpec(memory_space=pltpu.SMEM), pl.BlockSpec(memory_space=pltpu.VMEM)],
        out_specs=(hbm, hbm, hbm),
        scratch_shapes=scratch,
        compiler_params=pltpu.CompilerParams(
            collective_id=0, has_side_effects=True, vmem_limit_bytes=48 * 1024 * 1024
        ),
    )(
        mesh_in,
        grid_in,
        cotangent,
        w_send,
        w_self,
        w_out,
        w_src,
        w_dst,
        w_dec,
        adj_blocks,
        adj_index,
        idx,
    )


def solution(mesh):
    rows = P(("groups", "blk"), None)
    return jax.shard_map(
        body,
        mesh=mesh,
        in_specs=(rows,) * 3
        + (P(),) * 6
        + (
            P("blk", None, None, None),
            P(),
            P("blk", None, None),
            P("blk", None, None),
            P("blk", None),
        ),
        out_specs=(rows, rows, rows),
        check_vma=False,
    )
```

time: 115 us -> 63.9 us (0.56)
  Pallas kernels: 0 us -> 49.2 us
  starting transfers between devices: 35.1 us -> 0 us
  waiting for transfers between devices: 29.8 us -> 0 us
  other arithmetic: 16.1 us -> 0.84 us
  matrix products: 14.3 us -> 0 us
  local copies, waits for them, and re-layouts: 17.7 us -> 12.6 us
    pallas_call x0 -> x1, Pallas kernels: none -> 49.2 us  [body(): pl.pallas_call(functools.partial(kernel, n), out_shape=(jax.ShapeDtypeStr...]
    ppermute x20 -> x0, starting transfers between devices: 35.1 us -> none  [passed_along(): return lax.ppermute(block, axis, route)]
    ppermute x20 -> x0, waiting for transfers between devices: 29.8 us -> none  [passed_along(): return lax.ppermute(block, axis, route)]
    dot_general x14 -> x0, matrix products: 14.3 us -> none  [the longest x1 3.53 us: body(): jnp.einsum('wm,mjd->wjd', spots, contrib.reshape(blocks * neighbours, 128...]
    scatter-add x7 -> x0, other arithmetic: 13.3 us -> none  [the longest x5 7.36 us: body(): d_src_total = d_src_total.at[held[place]].add(back.astype(jnp.float32))]
    gather x8 -> x0, local copies, waits for them, and re-layouts: 9.1 us -> none  [the longest x5 3.51 us: body(): rows_out = src_proj[held[place]]]
    unnamed x68 -> x25, local copies, waits for them, and re-layouts: 4.13 us -> 12.6 us
    reshape x1, local copies, waits for them, and re-layouts: 2.07 us -> 0.07 us  [body(): jnp.pad(dst, ((0, 11), (0, 0)), constant_values=-1).reshape(1, 8, 2 * slots)]
  transfers between devices with their start and end apart: 20 -> 0, of which waited for: 9 -> 0; matrix products, arithmetic and copies ran while one was open for 21% -> 0% of each run, Pallas kernels for 0% -> 0%
where the time goes in v1:
time: 63.9 us; the launch traced here: 63.4 us
  Pallas kernels  49.2 us (77%)
  local copies, waits for them, and re-layouts  12.6 us (20%)
  other arithmetic  0.84 us (1%)
  between operations  0.66 us (1%)
    pallas_call x1, Pallas kernels, body(): pl.pallas_call(functools.partial(kernel, n), out_shape=(jax.ShapeDtypeStr...  49.2 us
    unnamed x25, local copies, waits for them, and re-layouts  12.6 us

profile of v1, /device:TPU:0, one launch (start us, length us, event | category | flops | bytes accessed | tf_op | source)
XLA Modules:
  0.0 63.4 jit_solution(7029664382188926155)
XLA Ops:
  0.6 0.0 copy-start.8
  0.6 0.7 %copy.22 = s32[1,5,64]{2,1,0:T(8,128)S(1)} copy(s32[1,5,64]{2,0,1:T(1,128)} %param.25) | data formatting | bytes 2560
  1.4 0.1 pad_add_fusion.1
  1.4 0.8 %bitcast_select_fusion = s32[5,64]{1,0:T(8,128)S(1)} fusion(s32[1,5,64]{2,0,1:T(1,128)} %param.26, s32[5]{0:T(128)} %bitcast.7), kind=kLoop, calls=%fused_computation.2 | loop fusion | flops 640 | bytes 2580 | tf_op jit(solution)/shard_map/jit(_where)/select_n | solution.py:480
  2.2 0.1 reshape.11
  2.3 0.8 %copy.17.adj_index = s32[32,4]{1,0:T(8,128)S(1)} copy(s32[32,4]{0,1:T(4,128)} %param.24) | data formatting | bytes 1024 | tf_op args[10]
  3.0 0.0 copy-done.8
  3.0 0.0 copy-start
  3.0 1.0 %copy-done = bf16[512,512]{1,0:T(8,128)(2,1)S(1)} copy-done((bf16[512,512]{1,0:T(8,128)(2,1)S(1)}, bf16[512,512]{1,0:T(8,128)(2,1)}, u32[]{:S(2)}) %copy-start) | copy-done | bytes 524312
  4.1 0.0 copy-start.1
  4.1 1.0 %copy-done.1 = bf16[512,512]{1,0:T(8,128)(2,1)S(1)} copy-done((bf16[512,512]{1,0:T(8,128)(2,1)S(1)}, bf16[512,512]{1,0:T(8,128)(2,1)}, u32[]{:S(2)}) %copy-start.1) | copy-done | bytes 524312
  5.1 0.0 copy-start.2
  5.1 1.0 %copy-done.2 = bf16[512,512]{1,0:T(8,128)(2,1)S(1)} copy-done((bf16[512,512]{1,0:T(8,128)(2,1)S(1)}, bf16[512,512]{1,0:T(8,128)(2,1)}, u32[]{:S(2)}) %copy-start.2) | copy-done | bytes 524312
  6.2 0.0 copy-start.3
  6.2 1.0 %copy-done.3 = bf16[512,512]{1,0:T(8,128)(2,1)S(1)} copy-done((bf16[512,512]{1,0:T(8,128)(2,1)S(1)}, bf16[512,512]{1,0:T(8,128)(2,1)}, u32[]{:S(2)}) %copy-start.3) | copy-done | bytes 524312
  7.2 0.0 copy-start.4
  7.2 1.0 %copy-done.4 = bf16[512,512]{1,0:T(8,128)(2,1)S(1)} copy-done((bf16[512,512]{1,0:T(8,128)(2,1)S(1)}, bf16[512,512]{1,0:T(8,128)(2,1)}, u32[]{:S(2)}) %copy-start.4) | copy-done | bytes 524312
  8.3 0.0 copy-start.5
  8.3 1.0 %copy-done.5 = bf16[512,512]{1,0:T(8,128)(2,1)S(1)} copy-done((bf16[512,512]{1,0:T(8,128)(2,1)S(1)}, bf16[512,512]{1,0:T(8,128)(2,1)}, u32[]{:S(2)}) %copy-start.5) | copy-done | bytes 524312
  9.3 0.0 copy-start.6
  9.3 0.9 %copy-done.6 = bf16[256,512]{1,0:T(8,128)(2,1)S(1)} copy-done((bf16[256,512]{1,0:T(8,128)(2,1)S(1)}, bf16[256,512]{1,0:T(8,128)(2,1)}, u32[]{:S(2)}) %copy-start.6) | copy-done | bytes 262168
  10.3 0.0 copy-start.7
  10.3 0.9 %copy-done.7 = bf16[2,4,128,128]{3,2,1,0:T(8,128)(2,1)S(1)} copy-done((bf16[2,4,128,128]{3,2,1,0:T(8,128)(2,1)S(1)}, bf16[2,4,128,128]{3,2,1,0:T(8,128)(2,1)}, u32[]{:S(2)}) %copy-start.7) | copy-done | bytes 262168
  11.2 0.0 copy-start.9
  11.2 0.9 %copy-done.9 = bf16[128,512]{1,0:T(8,128)(2,1)S(1)} copy-done((bf16[128,512]{1,0:T(8,128)(2,1)S(1)}, bf16[128,512]{1,0:T(8,128)(2,1)}, u32[]{:S(2)}) %copy-start.9) | copy-done | bytes 131096
  12.1 49.2 %shard_map.157 = (bf16[128,512]{1,0:T(8,128)(2,1)S(1)}, bf16[128,512]{1,0:T(8,128)(2,1)S(1)}, bf16[256,512]{1,0:T(8,128)(2,1)S(1)}) custom-call(bf16[256,512]{1,0:T(8,128)(2,1)S(1)} %copy-done.6, bf16[128,512]{1,0:T(8,128)(2,1)S(1)} %copy-done.8, bf16[128,512]{1,0:T(8,128)(2,1)S(1)} %copy-done.9, bf16[512,512]{1,0:T(8,128)(2,1)S(1)} %copy-done, ...), custom_call_target="tpu_custom_call" | custom-call | tf_op jit(solution)/shard_map/pallas_call | solution.py:552
  61.4 0.7 %copy.26 = bf16[128,512]{1,0:T(8,128)(2,1)} copy(bf16[128,512]{1,0:T(8,128)(2,1)S(1)} %get-tuple-element.6) | data formatting | bytes 262144
  62.0 0.7 %copy.27 = bf16[128,512]{1,0:T(8,128)(2,1)} copy(bf16[128,512]{1,0:T(8,128)(2,1)S(1)} %get-tuple-element.7) | data formatting | bytes 262144
  62.7 0.7 %copy.28 = bf16[256,512]{1,0:T(8,128)(2,1)} copy(bf16[256,512]{1,0:T(8,128)(2,1)S(1)} %get-tuple-element.8) | data formatting | bytes 524288
  (3 shorter events, 0.0 us)
Async XLA Ops:
  0.6 2.4 %copy-start.8 = (bf16[128,512]{1,0:T(8,128)(2,1)S(1)}, bf16[128,512]{1,0:T(8,128)(2,1)}, u32[]{:S(2)}) copy-start(bf16[128,512]{1,0:T(8,128)(2,1)} %grid_hbm.1) | copy-start | bytes 393220
  3.0 1.0 %copy-start = (bf16[512,512]{1,0:T(8,128)(2,1)S(1)}, bf16[512,512]{1,0:T(8,128)(2,1)}, u32[]{:S(2)}) copy-start(bf16[512,512]{1,0:T(8,128)(2,1)} %w_send_hbm.1) | copy-start | bytes 1572868
  4.1 1.0 %copy-start.1 = (bf16[512,512]{1,0:T(8,128)(2,1)S(1)}, bf16[512,512]{1,0:T(8,128)(2,1)}, u32[]{:S(2)}) copy-start(bf16[512,512]{1,0:T(8,128)(2,1)} %w_self_hbm.1) | copy-start | bytes 1572868
  5.1 1.0 %copy-start.2 = (bf16[512,512]{1,0:T(8,128)(2,1)S(1)}, bf16[512,512]{1,0:T(8,128)(2,1)}, u32[]{:S(2)}) copy-start(bf16[512,512]{1,0:T(8,128)(2,1)} %w_out_hbm.1) | copy-start | bytes 1572868
  6.2 1.0 %copy-start.3 = (bf16[512,512]{1,0:T(8,128)(2,1)S(1)}, bf16[512,512]{1,0:T(8,128)(2,1)}, u32[]{:S(2)}) copy-start(bf16[512,512]{1,0:T(8,128)(2,1)} %w_src_hbm.1) | copy-start | bytes 1572868
  7.2 1.0 %copy-start.4 = (bf16[512,512]{1,0:T(8,128)(2,1)S(1)}, bf16[512,512]{1,0:T(8,128)(2,1)}, u32[]{:S(2)}) copy-start(bf16[512,512]{1,0:T(8,128)(2,1)} %w_dst_hbm.1) | copy-start | bytes 1572868
  8.3 1.0 %copy-start.5 = (bf16[512,512]{1,0:T(8,128)(2,1)S(1)}, bf16[512,512]{1,0:T(8,128)(2,1)}, u32[]{:S(2)}) copy-start(bf16[512,512]{1,0:T(8,128)(2,1)} %w_dec_hbm.1) | copy-start | bytes 1572868
  9.3 0.9 %copy-start.6 = (bf16[256,512]{1,0:T(8,128)(2,1)S(1)}, bf16[256,512]{1,0:T(8,128)(2,1)}, u32[]{:S(2)}) copy-start(bf16[256,512]{1,0:T(8,128)(2,1)} %mesh_hbm.1) | copy-start | bytes 786436
  10.3 0.9 %copy-start.7 = (bf16[2,4,128,128]{3,2,1,0:T(8,128)(2,1)S(1)}, bf16[2,4,128,128]{3,2,1,0:T(8,128)(2,1)}, u32[]{:S(2)}) copy-start(bf16[2,4,128,128]{3,2,1,0:T(8,128)(2,1)} %adj_hbm.1) | copy-start | bytes 786436
  11.2 0.9 %copy-start.9 = (bf16[128,512]{1,0:T(8,128)(2,1)S(1)}, bf16[128,512]{1,0:T(8,128)(2,1)}, u32[]{:S(2)}) copy-start(bf16[128,512]{1,0:T(8,128)(2,1)} %cot_hbm.1) | copy-start | bytes 393220

commit v2 on v1

--- a/solution.py
+++ b/solution.py
@@ -38,8 +38,10 @@
     w_dst_hbm,
     w_dec_hbm,
     adj_hbm,
-    adj_index,
-    idx,
+    adj_index_hbm,
+    src_rows,
+    dst_rows,
+    counts,
     grid_out_hbm,
     grad_grid_hbm,
     grad_mesh_hbm,
@@ -53,6 +55,8 @@
     w_dst,
     w_dec,
     adj,
+    adj_index,
+    idx,
     nb,
     pre,
     win,
@@ -139,6 +143,7 @@
         (w_dec_hbm, w_dec),
         (w_out_hbm, w_out),
         (w_src_hbm, w_src),
+        (adj_index_hbm, adj_index),
     ]
     loads = [pltpu.make_async_copy(a, b, load_sem.at[i]) for i, (a, b) in enumerate(pairs)]
     for copy in loads:
@@ -185,6 +190,17 @@
         panel(c, 0, 2, 0, y_mate)
         panel(c, 0, 1, 1, mate)
 
+    spot = lax.broadcasted_iota(jnp.int32, (1, 64), 1)
+    idx[5] = jnp.full((8, 128), -1, jnp.int32)
+    for place in range(2 * REACH + 1):
+        row = jnp.broadcast_to(src_rows[0, place : place + 1, :], (8, 64))
+        idx[place, :, 0:64] = row
+        idx[place, :, 64:128] = row
+        alive = spot < counts[0:1, place : place + 1]
+        column = place % 2 * 64
+        idx[5, place // 2 : place // 2 + 1, column : column + 64] = jnp.where(
+            alive, dst_rows[0, place : place + 1, :], -1
+        )
     idx_copies = []
     for place in range(2 * REACH + 1):
         if place != REACH:
@@ -203,6 +219,7 @@
         panel(c, passed, 4, 3, mate)
 
     loads[2].wait()
+    loads[10].wait()
     for b in range(blocks):
         slots = []
         for k in range(neighbours):
@@ -472,15 +489,7 @@
     n = lax.axis_size("blk")
     per_dev, width = mesh_in.shape
     grid_rows = grid_in.shape[0]
-    places, slots = src_rows.shape[1], src_rows.shape[2]
     cw, ew = width // CHUNKS, width // EDGE_CHUNKS
-    src = jnp.concatenate([src_rows[0], src_rows[0]], axis=-1)
-    src = jnp.broadcast_to(src[:, None, :], (places, 8, 2 * slots))
-    alive = jnp.arange(slots, dtype=jnp.int32)[None, :] < counts[0][:, None]
-    dst = jnp.where(alive, dst_rows[0], -1)
-    dst = jnp.pad(dst, ((0, 11), (0, 0)), constant_values=-1).reshape(1, 8, 2 * slots)
-    idx = jnp.concatenate([src, dst], axis=0)
-
     def vmem(*shape, dtype=BF16):
         return pltpu.VMEM(shape, dtype)
 
@@ -498,6 +507,8 @@
         weight,
         weight,
         vmem(*adj_blocks.shape),
+        pltpu.SMEM(adj_index.shape, jnp.int32),
+        vmem(6, 8, 128, dtype=jnp.int32),
         vmem(per_dev, width),
         vmem(per_dev, width, dtype=F32),
         vmem(CHUNKS, 5, per_dev, cw),
@@ -531,7 +542,7 @@
         vmem(grid_rows, width),
         vmem(grid_rows, width),
         vmem(per_dev, width),
-        dma((10,)),
+        dma((11,)),
         dma((3,)),
         dma((5,)),
         dma((5,)),
@@ -548,7 +559,7 @@
         dma((CHUNKS,)),
         dma((CHUNKS,)),
     ]
-    hbm = pl.BlockSpec(memory_space=pl.ANY)
+    hbm = pl.BlockSpec(memory_space=pltpu.HBM)
     return pl.pallas_call(
         functools.partial(kernel, n),
         out_shape=(
@@ -556,12 +567,11 @@
             jax.ShapeDtypeStruct(grid_in.shape, BF16),
             jax.ShapeDtypeStruct(mesh_in.shape, BF16),
         ),
-        in_specs=[hbm] * 10
-        + [pl.BlockSpec(memory_space=pltpu.SMEM), pl.BlockSpec(memory_space=pltpu.VMEM)],
+        in_specs=[hbm] * 11 + [pl.BlockSpec(memory_space=pltpu.VMEM)] * 3,
         out_specs=(hbm, hbm, hbm),
         scratch_shapes=scratch,
         compiler_params=pltpu.CompilerParams(
-            collective_id=0, has_side_effects=True, vmem_limit_bytes=48 * 1024 * 1024
+            collective_id=0, has_side_effects=True, vmem_limit_bytes=64 * 1024 * 1024 - 65536
         ),
     )(
         mesh_in,
@@ -575,7 +585,9 @@
         w_dec,
         adj_blocks,
         adj_index,
-        idx,
+        src_rows,
+        dst_rows,
+        counts,
     )
 
 

time: 63.9 us -> 56.3 us (0.88)
  local copies, waits for them, and re-layouts: 12.6 us -> 5.64 us
  other arithmetic: 0.84 us -> 0 us
    unnamed x25 -> x14, local copies, waits for them, and re-layouts: 12.6 us -> 5.64 us
    select_n x1 -> x0, other arithmetic: 0.75 us -> none  [body(): dst = jnp.where(alive, dst_rows[0], -1)]
where the time goes in v2:
time: 56.3 us; the launch traced here: 56 us
  Pallas kernels  49.7 us (88%)
  local copies, waits for them, and re-layouts  5.64 us (10%)
  between operations  0.67 us (1%)
    pallas_call x1, Pallas kernels, body(): pl.pallas_call(functools.partial(kernel, n), out_shape=(jax.ShapeDtypeStr...  49.7 us
    unnamed x14, local copies, waits for them, and re-layouts  5.64 us

profile of v2, /device:TPU:0, one launch (start us, length us, event | category | flops | bytes accessed | tf_op | source)
XLA Modules:
  0.0 56.0 jit_solution(5765910165778563171)
XLA Ops:
  0.6 0.0 copy-start.2
  0.6 1.3 %copy.18.src_rows = s32[1,5,64]{2,1,0:T(8,128)} copy(s32[1,5,64]{2,0,1:T(1,128)} %param.25) | data formatting | bytes 2560 | tf_op args[11]
  1.9 0.0 copy-done.2
  1.9 0.0 copy-start.3
  1.9 0.6 %copy.19.dst_rows = s32[1,5,64]{2,1,0:T(8,128)} copy(s32[1,5,64]{2,0,1:T(1,128)S(1)} %copy-done.2) | data formatting | bytes 2560 | tf_op args[12]
  2.5 0.1 copy-done.3
  2.6 0.7 %copy.17.adj_index_hbm = s32[32,4]{1,0:T(8,128)} copy(s32[32,4]{0,1:T(4,128)S(1)} %copy-done.3) | data formatting | bytes 1024 | tf_op args[10]
  3.3 49.7 %shard_map.157 = (bf16[128,512]{1,0:T(8,128)(2,1)}, bf16[128,512]{1,0:T(8,128)(2,1)}, bf16[256,512]{1,0:T(8,128)(2,1)}) custom-call(bf16[256,512]{1,0:T(8,128)(2,1)} %mesh_hbm.1, bf16[128,512]{1,0:T(8,128)(2,1)} %grid_hbm.1, bf16[128,512]{1,0:T(8,128)(2,1)} %cot_hbm.1, bf16[512,512]{1,0:T(8,128)(2,1)} %w_send_hbm.1, bf16[512,512]{1,0:T(8,128)(2,1)} %w_self_hbm.1, ...), custom_call_target="tpu_custom_call" | custom-call | tf_op jit(solution)/shard_map/pallas_call | solution.py:563
  53.0 0.0 copy-start.1
  53.1 0.0 copy-start
  53.1 1.6 %copy.23 = bf16[128,512]{1,0:T(8,128)(2,1)} copy(bf16[128,512]{1,0:T(8,128)(2,1)} %get-tuple-element.6) | data formatting | bytes 262144
  54.7 0.0 copy-done.1
  54.7 0.7 %copy.24 = bf16[128,512]{1,0:T(8,128)(2,1)} copy(bf16[128,512]{1,0:T(8,128)(2,1)S(1)} %copy-done.1) | data formatting | bytes 262144
  55.3 0.0 copy-done
  55.3 0.7 %copy.25 = bf16[256,512]{1,0:T(8,128)(2,1)} copy(bf16[256,512]{1,0:T(8,128)(2,1)S(1)} %copy-done) | data formatting | bytes 524288
Async XLA Ops:
  0.6 1.3 %copy-start.2 = (s32[1,5,64]{2,0,1:T(1,128)S(1)}, s32[1,5,64]{2,0,1:T(1,128)}, u32[]{:S(2)}) copy-start(s32[1,5,64]{2,0,1:T(1,128)} %param.26) | copy-start | bytes 3844
  1.9 0.7 %copy-start.3 = (s32[32,4]{0,1:T(4,128)S(1)}, s32[32,4]{0,1:T(4,128)}, u32[]{:S(2)}) copy-start(s32[32,4]{0,1:T(4,128)} %param.24) | copy-start | bytes 1540
  53.0 1.6 %copy-start.1 = (bf16[128,512]{1,0:T(8,128)(2,1)S(1)}, bf16[128,512]{1,0:T(8,128)(2,1)}, u32[]{:S(2)}) copy-start(bf16[128,512]{1,0:T(8,128)(2,1)} %get-tuple-element.7) | copy-start | bytes 393220
  53.1 2.3 %copy-start = (bf16[256,512]{1,0:T(8,128)(2,1)S(1)}, bf16[256,512]{1,0:T(8,128)(2,1)}, u32[]{:S(2)}) copy-start(bf16[256,512]{1,0:T(8,128)(2,1)} %get-tuple-element.8) | copy-start | bytes 786436

commit v3 on v2

--- a/solution.py
+++ b/solution.py
@@ -265,12 +265,14 @@
     high = proj.astype(BF16)
     low = (proj - high.astype(F32)).astype(BF16)
     dproj[...] = mm(join[...], jnp.concatenate([high, low], axis=0))
-    if CHUNKS > 2:
-        hop_y(2)
-        hop_core(1)
+    hop_y(2)
+    hop_core(1)
     loads[6].wait()
     loads[7].wait()
     dsum[...] = mm(join[:, 0:128], mm_nt(cot[...], w_dec[...]).astype(BF16)).astype(BF16)
+
+    hop_y(3)
+    hop_core(2)
 
     for copy in idx_copies:
         copy.wait()
@@ -310,15 +312,8 @@
         return acc + mm(act, w_out[cols, :])
 
     acc = mesh[...].astype(F32)
-    done_y = min(3, CHUNKS) if CHUNKS > 2 else 2
-    done_core = done_y - 1
+    hop_core(3)
     for c in range(CHUNKS):
-        if done_y < CHUNKS:
-            hop_y(done_y)
-            done_y += 1
-        if done_core < CHUNKS:
-            hop_core(done_core)
-            done_core += 1
         acc = mesh_chunk(c, acc)
     mesh_out[...] = acc.astype(BF16)
 
@@ -439,20 +434,20 @@
         total = g_own[c] + k_in[c, 0].astype(F32) + y_in[c].astype(F32)
         return mm_nt(total.astype(BF16), w_send[:, c * cw : (c + 1) * cw])
 
-    acc = None
-    for step in range(CHUNKS + 3):
-        if step < CHUNKS:
-            spread(step)
-        if 0 <= step - 1 < CHUNKS:
-            fold_core(step - 1)
-        if 0 <= step - 2 < CHUNKS:
-            fold_z(step - 2)
-        if step == CHUNKS:
-            acc = mm_nt(d_pre[...], w_self[...])
-        if step == CHUNKS + 1:
-            for c in range(CHUNKS - 2):
-                acc += fold_y(c)
-    for c in range(max(CHUNKS - 2, 0), CHUNKS):
+    spread(0)
+    spread(1)
+    spread(2)
+    fold_core(0)
+    spread(3)
+    fold_core(1)
+    fold_core(2)
+    fold_z(0)
+    fold_core(3)
+    fold_z(1)
+    fold_z(2)
+    acc = mm_nt(d_pre[...], w_self[...])
+    fold_z(3)
+    for c in range(CHUNKS):
         acc += fold_y(c)
 
     h32 = mesh[...].astype(F32)

time: 56.3 us -> 54.3 us (0.964)
  Pallas kernels: 49.7 us -> 47.8 us
    pallas_call x1, Pallas kernels: 49.7 us -> 47.8 us  [body(): pl.pallas_call(functools.partial(kernel, n), out_shape=(jax.ShapeDtypeStr...]
where the time goes in v3:
time: 54.3 us; the launch traced here: 54.1 us
  Pallas kernels  47.8 us (88%)
  local copies, waits for them, and re-layouts  5.64 us (10%)
  between operations  0.67 us (1%)
    pallas_call x1, Pallas kernels, body(): pl.pallas_call(functools.partial(kernel, n), out_shape=(jax.ShapeDtypeStr...  47.8 us
    unnamed x14, local copies, waits for them, and re-layouts  5.64 us

profile of v3, /device:TPU:0, one launch (start us, length us, event | category | flops | bytes accessed | tf_op | source)
XLA Modules:
  0.0 54.1 jit_solution(15978048702923259497)
XLA Ops:
  0.6 0.0 copy-start.2
  0.6 1.3 %copy.18.src_rows = s32[1,5,64]{2,1,0:T(8,128)} copy(s32[1,5,64]{2,0,1:T(1,128)} %param.25) | data formatting | bytes 2560 | tf_op args[11]
  1.9 0.0 copy-done.2
  1.9 0.0 copy-start.3
  1.9 0.6 %copy.19.dst_rows = s32[1,5,64]{2,1,0:T(8,128)} copy(s32[1,5,64]{2,0,1:T(1,128)S(1)} %copy-done.2) | data formatting | bytes 2560 | tf_op args[12]
  2.5 0.1 copy-done.3
  2.6 0.7 %copy.17.adj_index_hbm = s32[32,4]{1,0:T(8,128)} copy(s32[32,4]{0,1:T(4,128)S(1)} %copy-done.3) | data formatting | bytes 1024 | tf_op args[10]
  3.3 47.8 %shard_map.157 = (bf16[128,512]{1,0:T(8,128)(2,1)}, bf16[128,512]{1,0:T(8,128)(2,1)}, bf16[256,512]{1,0:T(8,128)(2,1)}) custom-call(bf16[256,512]{1,0:T(8,128)(2,1)} %mesh_hbm.1, bf16[128,512]{1,0:T(8,128)(2,1)} %grid_hbm.1, bf16[128,512]{1,0:T(8,128)(2,1)} %cot_hbm.1, bf16[512,512]{1,0:T(8,128)(2,1)} %w_send_hbm.1, bf16[512,512]{1,0:T(8,128)(2,1)} %w_self_hbm.1, ...), custom_call_target="tpu_custom_call" | custom-call | tf_op jit(solution)/shard_map/pallas_call | solution.py:558
  51.1 0.0 copy-start.1
  51.1 0.0 copy-start
  51.1 1.6 %copy.23 = bf16[128,512]{1,0:T(8,128)(2,1)} copy(bf16[128,512]{1,0:T(8,128)(2,1)} %get-tuple-element.6) | data formatting | bytes 262144
  52.7 0.0 copy-done.1
  52.7 0.7 %copy.24 = bf16[128,512]{1,0:T(8,128)(2,1)} copy(bf16[128,512]{1,0:T(8,128)(2,1)S(1)} %copy-done.1) | data formatting | bytes 262144
  53.4 0.0 copy-done
  53.4 0.7 %copy.25 = bf16[256,512]{1,0:T(8,128)(2,1)} copy(bf16[256,512]{1,0:T(8,128)(2,1)S(1)} %copy-done) | data formatting | bytes 524288
Async XLA Ops:
  0.6 1.3 %copy-start.2 = (s32[1,5,64]{2,0,1:T(1,128)S(1)}, s32[1,5,64]{2,0,1:T(1,128)}, u32[]{:S(2)}) copy-start(s32[1,5,64]{2,0,1:T(1,128)} %param.26) | copy-start | bytes 3844
  1.9 0.7 %copy-start.3 = (s32[32,4]{0,1:T(4,128)S(1)}, s32[32,4]{0,1:T(4,128)}, u32[]{:S(2)}) copy-start(s32[32,4]{0,1:T(4,128)} %param.24) | copy-start | bytes 1540
  51.1 1.6 %copy-start.1 = (bf16[128,512]{1,0:T(8,128)(2,1)S(1)}, bf16[128,512]{1,0:T(8,128)(2,1)}, u32[]{:S(2)}) copy-start(bf16[128,512]{1,0:T(8,128)(2,1)} %get-tuple-element.7) | copy-start | bytes 393220
  51.1 2.3 %copy-start = (bf16[256,512]{1,0:T(8,128)(2,1)S(1)}, bf16[256,512]{1,0:T(8,128)(2,1)}, u32[]{:S(2)}) copy-start(bf16[256,512]{1,0:T(8,128)(2,1)} %get-tuple-element.8) | copy-start | bytes 786436
